TPU v7x, 32 devices: a whole 2x2x4 slice. The times are simulated.
32 devices in a mesh: face: 2 (over core), sub: 16 (over z, y, x).
Axes of the slice: x: 2, y: 2, z: 4, core: 2. Of those that a mesh axis runs over, the one named last changes fastest.
Arguments:
- features: bfloat16 [768, 24, 192], P(('face', 'sub')), may hold values from -6 to 6
- w_first: bfloat16 [3, 3, 192, 192], replicated, may hold values from -0.15625 to 0.15625
- b_first: float32 [192], replicated, may hold values from -3 to 3
- w_second: bfloat16 [3, 3, 192, 192], replicated, may hold values from -0.15625 to 0.15625
- neighbours: int32 [32, 4], replicated, may hold values from 0 to 31, as said below
- rotations: int32 [32, 4], replicated, may hold values from 0 to 3
- cotangent: bfloat16 [384, 12, 192], P(('face', 'sub')), may hold values from -6 to 6
Outputs:
- pooled: bfloat16 [384, 12, 192], P(('face', 'sub'))
- grad_input: bfloat16 [768, 24, 192], P(('face', 'sub'))
- grad_w1: float32 [3, 3, 192, 192], replicated
- grad_b1: float32 [192], replicated
- grad_w2: float32 [3, 3, 192, 192], replicated
Inputs may be any that keep to these rules, and one draw needn't show every extreme that they name: neighbours[d, e] is a tile f * 16 + s other than d; it has the same f as d or the same s as d; two tiles of the same f share at most one edge, and no tile names the same tile of its own f at two edges.
All inputs are finite; a program needn't handle non-finite values.
Results may differ from a plain program's by a relative error of at most 0.012.
Values may be sent and summed in bfloat16 or wider, within the bound.
A program may use at most 64 MiB of HBM per device.

v0:
```python
import math
import jax
import jax.numpy as jnp
import numpy as np
from jax import lax
from jax.sharding import PartitionSpec as P


def rim_lookup():
    return np.array(
        [
            [[0, 0], [1, 0], [2, 0], [3, 0]],
            [[1, 0], [2, 1], [3, 0], [0, 1]],
            [[2, 1], [3, 1], [0, 1], [1, 1]],
            [[3, 1], [0, 0], [1, 1], [2, 0]],
        ],
        np.int32,
    )


def edge_codes(rotations):
    lookup = rim_lookup()[:, [2, 3, 0, 1], :]
    quarters = rotations[:, :, None] == jnp.arange(4, dtype=jnp.int32)[None, None, :]
    anchor_tab = jnp.asarray(lookup[:, :, 0].T)
    flip_tab = jnp.asarray(lookup[:, :, 1].T)
    anchors = jnp.sum(jnp.where(quarters, anchor_tab[None], 0), axis=2).astype(jnp.int32)
    flip_codes = jnp.sum(jnp.where(quarters, flip_tab[None], 0), axis=2).astype(jnp.int32)
    return (anchors, flip_codes)


def layout(neighbours, rotations):
    sub_count = lax.axis_size("sub")
    face_count = lax.axis_size("face")
    face_id = lax.axis_index("face")
    sub_id = lax.axis_index("sub")
    device = face_id * sub_count + sub_id
    anchors, flip_codes = edge_codes(rotations)

    def by_face(table_in):
        return lax.dynamic_index_in_dim(
            table_in.reshape(face_count, sub_count, 4), sub_id, 1, keepdims=False
        )

    def by_block(table_in):
        return lax.dynamic_slice_in_dim(table_in, face_id * sub_count, sub_count, 0)

    return {
        "device": device,
        "face_id": face_id,
        "sub_count": sub_count,
        "mine_nbr": lax.dynamic_index_in_dim(neighbours, device, 0, keepdims=False),
        "mine_anchor": lax.dynamic_index_in_dim(anchors, device, 0, keepdims=False),
        "mine_flip": lax.dynamic_index_in_dim(flip_codes, device, 0, keepdims=False),
        "block_nbr": by_block(neighbours),
        "block_anchor": by_block(anchors),
        "block_flip": by_block(flip_codes),
        "cross_nbr": by_face(neighbours),
        "cross_anchor": by_face(anchors),
    }


def outer_rows(square):
    return jnp.stack([square[0], square[:, -1], square[-1], square[:, 0]], axis=0)


def border_rows(padded):
    return jnp.stack([padded[0, 1:-1], padded[1:-1, -1], padded[-1, 1:-1], padded[1:-1, 0]], axis=0)


def flip_where(rows_in, flag_vec):
    return jnp.where(flag_vec[:, None, None] == 1, rows_in[:, ::-1], rows_in)


def surround(square, picked):
    padded = jnp.pad(square, ((1, 1), (1, 1), (0, 0)))
    padded = padded.at[0, 1:-1].set(picked[0])
    padded = padded.at[1:-1, -1].set(picked[1])
    padded = padded.at[-1, 1:-1].set(picked[2])
    padded = padded.at[1:-1, 0].set(picked[3])
    return padded


def fetch_halo(square, layout_info):
    extent, channels = (square.shape[0], square.shape[2])
    sub_count = layout_info["sub_count"]
    mine_nbr = layout_info["mine_nbr"]
    mine_anchor = layout_info["mine_anchor"]
    mine_flip = layout_info["mine_flip"]
    same_face = mine_nbr // sub_count == layout_info["face_id"]
    own_rows = outer_rows(square)
    from_face = lax.all_gather(own_rows[None], "face", axis=0, tiled=True).reshape(
        -1, extent * channels
    )
    face_slots = mine_nbr // sub_count * 4 + mine_anchor
    face_pick = (
        face_slots[:, None] == jnp.arange(from_face.shape[0], dtype=jnp.int32)[None, :]
    ) & jnp.logical_not(same_face)[:, None]
    across = jnp.dot(face_pick.astype(jnp.bfloat16), from_face, preferred_element_type=jnp.float32)
    from_block = lax.all_gather(own_rows[None], "sub", axis=0, tiled=True).reshape(
        -1, extent * channels
    )
    block_slots = mine_nbr % sub_count * 4 + mine_anchor
    block_pick = (
        block_slots[:, None] == jnp.arange(from_block.shape[0], dtype=jnp.int32)[None, :]
    ) & same_face[:, None]
    inside = jnp.dot(
        block_pick.astype(jnp.bfloat16), from_block, preferred_element_type=jnp.float32
    )
    picked = flip_where(
        (inside + across).astype(jnp.bfloat16).reshape(4, extent, channels), mine_flip
    )
    return picked


def return_halo(summed, layout_info):
    extent, channels = (summed.shape[0] - 2, summed.shape[2])
    device = layout_info["device"]
    border_ids = jnp.arange(4, dtype=jnp.int32)[None, None, :]
    own_rows = flip_where(border_rows(summed), layout_info["mine_flip"])
    from_face = (
        lax.all_gather(own_rows[None].astype(jnp.bfloat16), "face", axis=0, tiled=True)
        .astype(jnp.float32)
        .reshape(-1, extent * channels)
    )
    cross_mask = (layout_info["cross_nbr"] == device)[:, :, None] & (
        layout_info["cross_anchor"][:, :, None] == border_ids
    )
    arrived = lax.dot_general(
        cross_mask.reshape(-1, 4).astype(jnp.float32),
        from_face,
        (((0,), (0,)), ((), ())),
        precision=lax.Precision.HIGHEST,
        preferred_element_type=jnp.float32,
    )
    block_hits = (layout_info["block_nbr"] == device)[:, :, None] & (
        layout_info["block_anchor"][:, :, None] == border_ids
    )
    from_block = (
        lax.all_gather(own_rows[None].astype(jnp.bfloat16), "sub", axis=0, tiled=True)
        .astype(jnp.float32)
        .reshape(-1, extent * channels)
    )
    block_mask = block_hits.reshape(-1, 4).astype(jnp.float32)
    arrived = arrived + lax.dot_general(
        block_mask,
        from_block,
        (((0,), (0,)), ((), ())),
        precision=lax.Precision.HIGHEST,
        preferred_element_type=jnp.float32,
    )
    arrived = arrived.reshape(4, extent, channels)
    middle = summed[1:-1, 1:-1]
    middle = middle.at[0].add(arrived[0])
    middle = middle.at[:, -1].add(arrived[1])
    middle = middle.at[-1].add(arrived[2])
    middle = middle.at[:, 0].add(arrived[3])
    return middle


def gather_windows(padded, extent):
    portions = []
    for row_off in range(3):
        for col_off in range(3):
            portions.append(
                padded[row_off : row_off + extent, col_off : col_off + extent].reshape(
                    extent * extent, -1
                )
            )
    return jnp.concatenate(portions, axis=1)


def scatter_windows(spread, extent, channels):
    summed = jnp.zeros((extent + 2, extent + 2, channels), jnp.float32)
    for row_off in range(3):
        for col_off in range(3):
            offset_id = 3 * row_off + col_off
            portion = spread[:, offset_id * channels : (offset_id + 1) * channels].reshape(
                extent, extent, channels
            )
            summed = summed.at[row_off : row_off + extent, col_off : col_off + extent].add(portion)
    return summed


def local(features, w_first, b_first, w_second, neighbours, rotations, cotangent):
    extent, channels = (features.shape[1], features.shape[2])
    half_side = extent // 2
    layout_info = layout(neighbours, rotations)
    first_flat = w_first.reshape(9 * channels, channels)
    second_flat = w_second.reshape(9 * channels, channels)
    padded_in = surround(features, fetch_halo(features, layout_info))
    windows_in = gather_windows(padded_in, extent)
    hidden = jnp.dot(windows_in, first_flat, preferred_element_type=jnp.float32) + b_first
    active = jax.nn.silu(hidden).astype(jnp.bfloat16).reshape(extent, extent, channels)
    padded_act = surround(active, fetch_halo(active, layout_info))
    windows_act = gather_windows(padded_act, extent)
    second = jnp.dot(windows_act, second_flat, preferred_element_type=jnp.float32)
    summed_out = features.reshape(extent * extent, channels).astype(jnp.float32) + second
    pooled = (
        summed_out.reshape(half_side, 2, half_side, 2, channels)
        .mean(axis=(1, 3))
        .astype(jnp.bfloat16)
    )
    upward = (cotangent.astype(jnp.float32) * 0.25).astype(jnp.bfloat16)
    grad_out = jnp.broadcast_to(upward[:, None, :, None, :], (half_side, 2, half_side, 2, channels))
    grad_out = grad_out.reshape(extent * extent, channels)
    contract_rows = (((0,), (0,)), ((), ()))
    contract_cols = (((1,), (1,)), ((), ()))
    sum_w2 = lax.dot_general(
        windows_act, grad_out, contract_rows, preferred_element_type=jnp.float32
    )
    spread_two = lax.dot_general(
        grad_out, second_flat, contract_cols, preferred_element_type=jnp.float32
    )
    grad_active = return_halo(scatter_windows(spread_two, extent, channels), layout_info).astype(
        jnp.bfloat16
    )
    sigmoid_h = jax.nn.sigmoid(hidden)
    grad_hidden = (
        grad_active.reshape(extent * extent, channels).astype(jnp.float32)
        * sigmoid_h
        * (1.0 + hidden * (1.0 - sigmoid_h))
    )
    grad_hidden = grad_hidden.astype(jnp.bfloat16)
    sum_b1 = jnp.sum(grad_hidden, axis=0, dtype=jnp.float32)
    sum_w1 = lax.dot_general(
        windows_in, grad_hidden, contract_rows, preferred_element_type=jnp.float32
    )
    spread_one = lax.dot_general(
        grad_hidden, first_flat, contract_cols, preferred_element_type=jnp.float32
    )
    grad_input = return_halo(scatter_windows(spread_one, extent, channels), layout_info)
    grad_input = (
        grad_input + grad_out.astype(jnp.float32).reshape(extent, extent, channels)
    ).astype(jnp.bfloat16)
    total_w1, total_b1, total_w2 = lax.psum((sum_w1, sum_b1, sum_w2), ("face", "sub"))
    grad_scale = 1.0 / math.sqrt(neighbours.shape[0] * extent * extent)
    return (
        pooled,
        grad_input,
        (total_w1 * grad_scale).reshape(3, 3, channels, channels),
        total_b1 * grad_scale,
        (total_w2 * grad_scale).reshape(3, 3, channels, channels),
    )


def solution(mesh):
    in_specs = (
        P(("face", "sub"), None, None),
        P(),
        P(),
        P(),
        P(),
        P(),
        P(("face", "sub"), None, None),
    )
    out_specs = (P(("face", "sub"), None, None), P(("face", "sub"), None, None), P(), P(), P())
    return jax.shard_map(local, mesh=mesh, in_specs=in_specs, out_specs=out_specs, check_vma=False)
```

profile of v0, /device:TPU:0, one launch (start us, length us, event | category | flops | bytes accessed | tf_op | source)
XLA Modules:
  0.0 460.5 jit_solution(812224152784849294)
XLA Ops:
  11.3 2.4 fusion.49
  17.3 6.1 %scatter-add.89 = f32[26,26,192]{2,0,1:T(8,128)S(1)} dynamic-update-slice(f32[26,26,192]{2,0,1:T(8,128)S(1)} %scatter-add.86, f32[24,24,192]{2,0,1:T(8,128)S(1)} %copy_add_fusion.2, s32[]{:T(128)} %bitcast.3, s32[]{:T(128)} %bitcast.4, s32[]{:T(128)} %constant.897.clone.1) | dynamic-update-slice | bytes 884740 | tf_op jit(solution)/shard_map/scatter-add | solution.py:180
  23.4 3.1 add_select_fusion.1
  26.5 6.0 %scatter-add.90 = f32[26,26,192]{2,0,1:T(8,128)S(1)} dynamic-update-slice(f32[26,26,192]{2,0,1:T(8,128)S(1)} %scatter-add.89, f32[24,24,192]{2,0,1:T(8,128)S(1)} %add_select_fusion.1, s32[]{:T(128)} %bitcast.34, s32[]{:T(128)} %bitcast.35, s32[]{:T(128)} %constant.897.clone.1) | dynamic-update-slice | bytes 884740 | tf_op jit(solution)/shard_map/scatter-add | solution.py:180
  33.8 5.1 %scatter-add.91 = f32[26,26,192]{2,0,1:T(8,128)S(1)} dynamic-update-slice(f32[26,26,192]{2,0,1:T(8,128)S(1)} %scatter-add.90, f32[24,24,192]{2,0,1:T(8,128)S(1)} %slice_add_fusion.11, s32[]{:T(128)} %constant.903.clone.1, s32[]{:T(128)} %constant.897.clone.1, s32[]{:T(128)} %constant.897.clone.1) | dynamic-update-slice | bytes 884740 | tf_op jit(solution)/shard_map/scatter-add | solution.py:180
  40.2 4.9 %scatter-add.94 = f32[26,26,192]{2,0,1:T(8,128)S(1)} dynamic-update-slice(f32[26,26,192]{2,0,1:T(8,128)S(1)} %scatter-add.91, f32[24,24,192]{2,0,1:T(8,128)S(1)} %slice_add_fusion.10, s32[]{:T(128)} %constant.903.clone.1, s32[]{:T(128)} %constant.903.clone.1, s32[]{:T(128)} %constant.897.clone.1) | dynamic-update-slice | bytes 884740 | tf_op jit(solution)/shard_map/scatter-add | solution.py:180
  46.4 4.8 %scatter-add.95 = f32[26,26,192]{2,0,1:T(8,128)S(1)} dynamic-update-slice(f32[26,26,192]{2,0,1:T(8,128)S(1)} %scatter-add.94, f32[24,24,192]{2,0,1:T(8,128)S(1)} %slice_add_fusion.9, s32[]{:T(128)} %constant.903.clone.1, s32[]{:T(128)} %constant.911.clone.1, s32[]{:T(128)} %constant.897.clone.1) | dynamic-update-slice | bytes 884740 | tf_op jit(solution)/shard_map/scatter-add | solution.py:180
  52.5 5.1 %scatter-add.96 = f32[26,26,192]{2,0,1:T(8,128)S(1)} dynamic-update-slice(f32[26,26,192]{2,0,1:T(8,128)S(1)} %scatter-add.95, f32[24,24,192]{2,0,1:T(8,128)S(1)} %slice_add_fusion.8, s32[]{:T(128)} %constant.911.clone.1, s32[]{:T(128)} %constant.897.clone.1, s32[]{:T(128)} %constant.897.clone.1) | dynamic-update-slice | bytes 884740 | tf_op jit(solution)/shard_map/scatter-add | solution.py:180
  58.9 4.9 %scatter-add.99 = f32[26,26,192]{2,0,1:T(8,128)S(1)} dynamic-update-slice(f32[26,26,192]{2,0,1:T(8,128)S(1)} %scatter-add.96, f32[24,24,192]{2,0,1:T(8,128)S(1)} %slice_add_fusion.7, s32[]{:T(128)} %constant.911.clone.1, s32[]{:T(128)} %constant.903.clone.1, s32[]{:T(128)} %constant.897.clone.1) | dynamic-update-slice | bytes 884740 | tf_op jit(solution)/shard_map/scatter-add | solution.py:180
  64.1 4.8 %scatter-add.100 = f32[26,26,192]{2,0,1:T(8,128)S(1)} dynamic-update-slice(f32[26,26,192]{2,0,1:T(8,128)S(1)} %scatter-add.99, f32[24,24,192]{2,0,1:T(8,128)S(1)} %slice_add_fusion.6, s32[]{:T(128)} %constant.911.clone.1, s32[]{:T(128)} %constant.911.clone.1, s32[]{:T(128)} %constant.897.clone.1) | dynamic-update-slice | bytes 884740 | tf_op jit(solution)/shard_map/scatter-add | solution.py:180
  70.8 47.0 %all-gather = bf16[64,24,192]{2,1,0:T(8,128)(2,1)S(1)} all-gather(bf16[4,24,192]{2,1,0:T(8,128)(2,1)S(1)} %pad_maximum_fusion.2), channel_id=2, replica_groups=mesh['face'=2,'sub'=16] {'sub'}, dimensions={0}, use_global_device_ids=true | all-gather | bytes 626688 | tf_op jit(solution)/shard_map/all_gather | solution.py:99
  127.7 39.7 %all-gather.5 = bf16[64,24,192]{2,1,0:T(8,128)(2,1)S(1)} all-gather(bf16[4,24,192]{2,1,0:T(8,128)(2,1)S(1)} %get-tuple-element.535), channel_id=7, replica_groups=mesh['face'=2,'sub'=16] {'sub'}, dimensions={0}, use_global_device_ids=true | all-gather | bytes 626688 | tf_op jit(solution)/shard_map/all_gather | solution.py:139
  181.9 3.8 concatenate.84
  185.7 3.4 convert_reduce_fusion
  196.8 44.8 %all-gather.2 = bf16[64,24,192]{2,1,0:T(8,128)(2,1)} all-gather(bf16[4,24,192]{2,1,0:T(8,128)(2,1)S(1)} %pad_maximum_fusion.3), channel_id=4, replica_groups=mesh['face'=2,'sub'=16] {'sub'}, dimensions={0}, use_global_device_ids=true | all-gather | bytes 626688 | tf_op jit(solution)/shard_map/all_gather | solution.py:99
  246.2 2.1 fusion.48
  250.0 6.1 %scatter-add.110 = f32[26,26,192]{2,0,1:T(8,128)S(1)} dynamic-update-slice(f32[26,26,192]{2,0,1:T(8,128)S(1)} %scatter-add.109, f32[24,24,192]{2,0,1:T(8,128)S(1)} %copy_add_fusion.1, s32[]{:T(128)} %bitcast.3, s32[]{:T(128)} %bitcast.4, s32[]{:T(128)} %constant.897.clone.1) | dynamic-update-slice | bytes 884740 | tf_op jit(solution)/shard_map/scatter-add | solution.py:180
  256.1 3.1 add_select_fusion
  259.2 6.0 %scatter-add.111 = f32[26,26,192]{2,0,1:T(8,128)S(1)} dynamic-update-slice(f32[26,26,192]{2,0,1:T(8,128)S(1)} %scatter-add.110, f32[24,24,192]{2,0,1:T(8,128)S(1)} %add_select_fusion, s32[]{:T(128)} %bitcast.34, s32[]{:T(128)} %bitcast.35, s32[]{:T(128)} %constant.897.clone.1) | dynamic-update-slice | bytes 884740 | tf_op jit(solution)/shard_map/scatter-add | solution.py:180
  266.5 5.1 %scatter-add.114 = f32[26,26,192]{2,0,1:T(8,128)S(1)} dynamic-update-slice(f32[26,26,192]{2,0,1:T(8,128)S(1)} %scatter-add.111, f32[24,24,192]{2,0,1:T(8,128)S(1)} %slice_add_fusion.5, s32[]{:T(128)} %constant.903.clone.1, s32[]{:T(128)} %constant.897.clone.1, s32[]{:T(128)} %constant.897.clone.1) | dynamic-update-slice | bytes 884740 | tf_op jit(solution)/shard_map/scatter-add | solution.py:180
  272.9 4.9 %scatter-add.115 = f32[26,26,192]{2,0,1:T(8,128)S(1)} dynamic-update-slice(f32[26,26,192]{2,0,1:T(8,128)S(1)} %scatter-add.114, f32[24,24,192]{2,0,1:T(8,128)S(1)} %slice_add_fusion.4, s32[]{:T(128)} %constant.903.clone.1, s32[]{:T(128)} %constant.903.clone.1, s32[]{:T(128)} %constant.897.clone.1) | dynamic-update-slice | bytes 884740 | tf_op jit(solution)/shard_map/scatter-add | solution.py:180
  278.1 4.8 %scatter-add.116 = f32[26,26,192]{2,0,1:T(8,128)S(1)} dynamic-update-slice(f32[26,26,192]{2,0,1:T(8,128)S(1)} %scatter-add.115, f32[24,24,192]{2,0,1:T(8,128)S(1)} %slice_add_fusion.3, s32[]{:T(128)} %constant.903.clone.1, s32[]{:T(128)} %constant.911.clone.1, s32[]{:T(128)} %constant.897.clone.1) | dynamic-update-slice | bytes 884740 | tf_op jit(solution)/shard_map/scatter-add | solution.py:180
  283.1 5.1 %scatter-add.119 = f32[26,26,192]{2,0,1:T(8,128)S(1)} dynamic-update-slice(f32[26,26,192]{2,0,1:T(8,128)S(1)} %scatter-add.116, f32[24,24,192]{2,0,1:T(8,128)S(1)} %slice_add_fusion.2, s32[]{:T(128)} %constant.911.clone.1, s32[]{:T(128)} %constant.897.clone.1, s32[]{:T(128)} %constant.897.clone.1) | dynamic-update-slice | bytes 884740 | tf_op jit(solution)/shard_map/scatter-add | solution.py:180
  288.4 4.9 %scatter-add.120 = f32[26,26,192]{2,0,1:T(8,128)S(1)} dynamic-update-slice(f32[26,26,192]{2,0,1:T(8,128)S(1)} %scatter-add.119, f32[24,24,192]{2,0,1:T(8,128)S(1)} %slice_add_fusion.1, s32[]{:T(128)} %constant.911.clone.1, s32[]{:T(128)} %constant.903.clone.1, s32[]{:T(128)} %constant.897.clone.1) | dynamic-update-slice | bytes 884740 | tf_op jit(solution)/shard_map/scatter-add | solution.py:180
  294.8 4.8 %scatter-add.121 = f32[26,26,192]{2,0,1:T(8,128)S(1)} dynamic-update-slice(f32[26,26,192]{2,0,1:T(8,128)S(1)} %scatter-add.120, f32[24,24,192]{2,0,1:T(8,128)S(1)} %slice_add_fusion, s32[]{:T(128)} %constant.911.clone.1, s32[]{:T(128)} %constant.911.clone.1, s32[]{:T(128)} %constant.897.clone.1) | dynamic-update-slice | bytes 884740 | tf_op jit(solution)/shard_map/scatter-add | solution.py:180
  306.1 3.8 concatenate.85
  312.5 46.0 %all-gather.7 = bf16[64,24,192]{2,1,0:T(8,128)(2,1)} all-gather(bf16[4,24,192]{2,1,0:T(8,128)(2,1)S(1)} %copy-done.9), channel_id=9, replica_groups=mesh['face'=2,'sub'=16] {'sub'}, dimensions={0}, use_global_device_ids=true | all-gather | bytes 626688 | tf_op jit(solution)/shard_map/all_gather | solution.py:139
  361.3 2.5 reshape.1470
  377.8 2.1 copy.335
  379.9 2.7 convolution_add_fusion.4
  384.7 37.5 %psum.22 = f32[192]{0:T(256)S(1)} all-reduce(f32[192]{0:T(256)S(1)} %copy-done.34), channel_id=1, replica_groups=mesh['face'=2,'sub'=16] {'face','sub'}, use_global_device_ids=true, to_apply=%region_6.7 | all-reduce | flops 192 | bytes 1536 | tf_op jit(solution)/shard_map/psum | solution.py:235
  423.4 23.8 %all-reduce.7.cloned.1.call-done = (f32[1728,192]{0,1:T(8,128)}, f32[1728,192]{0,1:T(8,128)}) async-done(((f32[1728,192]{0,1:T(8,128)}, f32[1728,192]{0,1:T(8,128)}), (f32[1728,192]{0,1:T(8,128)}, f32[1728,192]{0,1:T(8,128)})) %all-reduce.7.cloned.1.call-update) | async-done | bytes 2654224 | tf_op jit(solution)/shard_map/psum | solution.py:235
  (239 shorter events, 94.4 us)
Async XLA Ops:
  7.2 178.5 %copy-start = (bf16[3,3,192,192]{3,2,1,0:T(8,128)(2,1)S(1)}, bf16[3,3,192,192]{3,2,1,0:T(8,128)(2,1)}, u32[]{:S(2)}) copy-start(bf16[3,3,192,192]{3,2,1,0:T(8,128)(2,1)} %param.78) | copy-start | bytes 1990660
  7.2 440.0 %all-reduce.7.cloned.1.call-start = ((), (), s32[]{:S(2)}) async-start(), calls=%async_computation | async-start | bytes 5505024 | tf_op jit(solution)/shard_map/psum | solution.py:235
  63.8 56.0 %copy-start.31 = (s32[32,4]{0,1:T(4,128)S(1)}, s32[32,4]{0,1:T(4,128)}, u32[]{:S(2)}) copy-start(s32[32,4]{0,1:T(4,128)} %param.82) | copy-start | bytes 1540
  63.8 56.0 %copy-start.32 = (s32[4,4]{1,0:T(4,128)S(1)}, s32[4,4]{1,0:T(4,128)}, u32[]{:S(2)}) copy-start(s32[4,4]{1,0:T(4,128)} %constant.917.clone) | copy-start | bytes 196
  63.9 56.0 %copy-start.33 = (s32[4,4]{1,0:T(4,128)S(1)}, s32[4,4]{1,0:T(4,128)}, u32[]{:S(2)}) copy-start(s32[4,4]{1,0:T(4,128)} %constant.918.clone) | copy-start | bytes 196
  63.9 56.7 %copy-start.17 = (s32[32,4]{0,1:T(4,128)S(1)}, s32[32,4]{0,1:T(4,128)}, u32[]{:S(2)}) copy-start(s32[32,4]{0,1:T(4,128)} %param.81) | copy-start | bytes 1540
  69.0 52.2 %copy-start.11 = (bf16[1,24,192]{2,1,0:T(8,128)(2,1)}, bf16[1,24,192]{2,1,0:T(8,128)(2,1)S(1)}, u32[]{:S(2)}) copy-start(bf16[1,24,192]{2,1,0:T(8,128)(2,1)S(1)} %get-tuple-element.494) | copy-start | bytes 27652
  69.0 52.2 %copy-start.12 = (bf16[1,24,192]{2,1,0:T(8,128)(2,1)}, bf16[1,24,192]{2,1,0:T(8,128)(2,1)S(1)}, u32[]{:S(2)}) copy-start(bf16[1,24,192]{2,1,0:T(8,128)(2,1)S(1)} %get-tuple-element.495) | copy-start | bytes 27652
  123.1 46.2 %copy-start.16 = (s32[32,4]{0,1:T(4,128)S(1)}, s32[32,4]{0,1:T(4,128)}, u32[]{:S(2)}) copy-start(s32[32,4]{0,1:T(4,128)} %copy-done.15) | copy-start | bytes 1540
  123.1 46.3 %copy-start.18 = (s32[32,4]{0,1:T(4,128)S(1)}, s32[32,4]{0,1:T(4,128)}, u32[]{:S(2)}) copy-start(s32[32,4]{0,1:T(4,128)} %param.81) | copy-start | bytes 1540
  124.0 3.7 copy-start.23
  124.0 3.7 copy-start.36
  126.8 43.7 %copy-start.19 = (pred[4]{0:T(512)(128)(4,1)}, pred[4]{0:T(512)(128)(4,1)S(1)}, u32[]{:S(2)}) copy-start(pred[4]{0:T(512)(128)(4,1)S(1)} %fusion.27) | copy-start | bytes 16
  175.4 4.8 %copy-start.4 = (f32[24,24,192]{2,0,1:T(8,128)S(1)}, f32[24,24,192]{2,0,1:T(8,128)}, u32[]{:S(2)}) copy-start(f32[24,24,192]{2,0,1:T(8,128)} %slice.1244) | copy-start | bytes 1327108
  177.3 2.2 copy-start.27
  179.7 2.1 copy-start.7
  181.9 3.8 copy-start.39
  288.4 11.2 %copy-start.6 = (bf16[576,192]{1,0:T(8,128)(2,1)S(1)}, bf16[576,192]{1,0:T(8,128)(2,1)}, u32[]{:S(2)}) copy-start(bf16[576,192]{1,0:T(8,128)(2,1)} %copy.330) | copy-start | bytes 663556
  293.3 6.4 %copy-start.3 = (bf16[64,24,192]{2,1,0:T(8,128)(2,1)S(1)}, bf16[64,24,192]{2,1,0:T(8,128)(2,1)}, u32[]{:S(2)}) copy-start(bf16[64,24,192]{2,1,0:T(8,128)(2,1)} %all-gather.2) | copy-start | bytes 1769476
  294.7 5.7 %copy-start.22 = (pred[4]{0:T(512)(128)(4,1)S(1)}, pred[4]{0:T(512)(128)(4,1)}, u32[]{:S(2)}) copy-start(pred[4]{0:T(512)(128)(4,1)} %get-tuple-element.468) | copy-start | bytes 16
  294.7 5.7 %copy-start.24 = (s32[4]{0:T(128)S(1)}, s32[4]{0:T(128)}, u32[]{:S(2)}) copy-start(s32[4]{0:T(128)} %copy-done.23) | copy-start | bytes 52
  294.8 6.0 %copy-start.10 = (bf16[8,24,192]{2,1,0:T(8,128)(2,1)S(1)}, bf16[8,24,192]{2,1,0:T(8,128)(2,1)}, u32[]{:S(2)}) copy-start(bf16[8,24,192]{2,1,0:T(8,128)(2,1)} %all-gather.3) | copy-start | bytes 221188
  294.8 6.1 %copy-start.35 = (pred[4]{0:T(512)(128)(4,1)S(1)}, pred[4]{0:T(512)(128)(4,1)}, u32[]{:S(2)}) copy-start(pred[4]{0:T(512)(128)(4,1)} %get-tuple-element.467) | copy-start | bytes 16
  294.8 6.1 %copy-start.37 = (s32[4]{0:T(128)S(1)}, s32[4]{0:T(128)}, u32[]{:S(2)}) copy-start(s32[4]{0:T(128)} %copy-done.36) | copy-start | bytes 52
  311.7 52.2 %copy-start.28 = (pred[8]{0:T(512)(128)(4,1)S(1)}, pred[8]{0:T(512)(128)(4,1)}, u32[]{:S(2)}) copy-start(pred[8]{0:T(512)(128)(4,1)} %copy-done.27) | copy-start | bytes 28
  311.8 52.2 %copy-start.30 = (s32[8]{0:T(128)S(1)}, s32[8]{0:T(128)}, u32[]{:S(2)}) copy-start(s32[8]{0:T(128)} %copy-done.29) | copy-start | bytes 100
  311.8 52.4 %copy-start.26 = (s32[64]{0:T(128)S(1)}, s32[64]{0:T(128)}, u32[]{:S(2)}) copy-start(s32[64]{0:T(128)} %copy-done.25) | copy-start | bytes 772
  360.4 12.9 %copy-start.8 = (f32[12,12,192]{2,1,0:T(8,128)S(1)}, f32[12,12,192]{2,1,0:T(8,128)}, u32[]{:S(2)}) copy-start(f32[12,12,192]{2,1,0:T(8,128)} %get-tuple-element.523) | copy-start | bytes 331780
  371.8 5.1 %copy-start.5 = (bf16[24,24,192]{2,1,0:T(8,128)(2,1)S(1)}, bf16[24,24,192]{2,1,0:T(8,128)(2,1)}, u32[]{:S(2)}) copy-start(bf16[24,24,192]{2,1,0:T(8,128)(2,1)} %param.77) | copy-start | bytes 663556
  374.6 5.2 %copy-start.2 = (bf16[3,3,192,192]{3,2,1,0:T(8,128)(2,1)S(1)}, bf16[3,3,192,192]{3,2,1,0:T(8,128)(2,1)}, u32[]{:S(2)}) copy-start(bf16[3,3,192,192]{3,2,1,0:T(8,128)(2,1)} %param.80) | copy-start | bytes 1990660
  382.6 2.1 copy-start.34
  450.4 3.3 copy-start.1
  (9 other events, 12.8 us)
Sparse Core Ops, SparseCore 0:
  311.9 135.2 all-reduce.6
where the time goes:
time: 463 us; the launch traced here: 460 us
  blocking collectives  223 us (48%)
  local copies, waits for them, and re-layouts  142 us (31%)
  other arithmetic  39.1 us (8%)
  waiting for transfers between devices  23.8 us (5%)
  matrix products  18 us (4%)
  between operations  15.1 us (3%)
    all_gather x2, blocking collectives, fetch_halo(): lax.all_gather(own_rows[None], 'sub', axis=0, tiled=True)  91.8 us
    all_gather x2, blocking collectives, return_halo(): lax.all_gather(own_rows[None].astype(jnp.bfloat16), 'sub', axis=0, tiled=...  85.7 us
    scatter-add x18, local copies, waits for them, and re-layouts, scatter_windows(): summed.at[row_off:row_off + extent, col_off:col_off + extent].add(portion)  83.3 us
    psum x1, blocking collectives, local(): lax.psum((sum_w1, sum_b1, sum_w2), ('face', 'sub'))  37.5 us
    psum x1, waiting for transfers between devices, local(): lax.psum((sum_w1, sum_b1, sum_w2), ('face', 'sub'))  23.8 us
    add x14, other arithmetic, scatter_windows(): summed.at[row_off:row_off + extent, col_off:col_off + extent].add(portion)  14.4 us
  transfers between devices with their start and end apart: 1, of which 1 were waited for; matrix products, arithmetic and copies ran while one was open for 6% of the time, Pallas kernels for 0%

commit v1 on v0

--- a/solution.py
+++ b/solution.py
@@ -232,7 +232,7 @@
     grad_input = (
         grad_input + grad_out.astype(jnp.float32).reshape(extent, extent, channels)
     ).astype(jnp.bfloat16)
-    total_w1, total_b1, total_w2 = lax.psum((sum_w1, sum_b1, sum_w2), ("face", "sub"))
+    total_w1, total_b1, total_w2 = lax.psum(lax.psum((sum_w1, sum_b1, sum_w2), "sub"), "face")
     grad_scale = 1.0 / math.sqrt(neighbours.shape[0] * extent * extent)
     return (
         pooled,

time: 463 us -> 537 us (1.16)
  waiting for transfers between devices: 23.8 us -> 90.5 us
  blocking collectives: 223 us -> 230 us
    psum x1 -> x2, waiting for transfers between devices: 23.8 us -> 90.5 us  [the longest x1 90.5 us: local(): lax.psum((sum_w1, sum_b1, sum_w2), 'sub')]
    psum x1 -> x2, blocking collectives: 37.5 us -> 42.8 us  [the longest x1 40.4 us: local(): lax.psum((sum_w1, sum_b1, sum_w2), 'sub')]
  transfers between devices with their start and end apart: 1 -> 2, of which waited for: 1 -> 1; matrix products, arithmetic and copies ran while one was open for 6% -> 5% of each run, Pallas kernels for 0% -> 0%
where the time goes in v1:
time: 537 us; the launch traced here: 535 us
  blocking collectives  230 us (43%)
  local copies, waits for them, and re-layouts  142 us (26%)
  waiting for transfers between devices  90.5 us (17%)
  other arithmetic  39.2 us (7%)
  matrix products  18 us (3%)
  between operations  15.2 us (3%)
    all_gather x2, blocking collectives, fetch_halo(): lax.all_gather(own_rows[None], 'sub', axis=0, tiled=True)  91.8 us
    psum x1, waiting for transfers between devices, local(): lax.psum((sum_w1, sum_b1, sum_w2), 'sub')  90.5 us
    all_gather x2, blocking collectives, return_halo(): lax.all_gather(own_rows[None].astype(jnp.bfloat16), 'sub', axis=0, tiled=...  87.6 us
    scatter-add x18, local copies, waits for them, and re-layouts, scatter_windows(): summed.at[row_off:row_off + extent, col_off:col_off + extent].add(portion)  83.4 us
    psum x1, blocking collectives, local(): lax.psum((sum_w1, sum_b1, sum_w2), 'sub')  40.4 us
    add x14, other arithmetic, scatter_windows(): summed.at[row_off:row_off + extent, col_off:col_off + extent].add(portion)  14.4 us
  transfers between devices with their start and end apart: 2, of which 1 were waited for; matrix products, arithmetic and copies ran while one was open for 5% of the time, Pallas kernels for 0%

profile of v1, /device:TPU:0, one launch (start us, length us, event | category | flops | bytes accessed | tf_op | source)
XLA Modules:
  0.0 534.7 jit_solution(10737096718554136030)
XLA Ops:
  11.3 2.4 fusion.49
  17.3 6.1 %scatter-add.89 = f32[26,26,192]{2,0,1:T(8,128)S(1)} dynamic-update-slice(f32[26,26,192]{2,0,1:T(8,128)S(1)} %scatter-add.86, f32[24,24,192]{2,0,1:T(8,128)S(1)} %copy_add_fusion.2, s32[]{:T(128)} %bitcast.3, s32[]{:T(128)} %bitcast.4, s32[]{:T(128)} %constant.897.clone.1) | dynamic-update-slice | bytes 884740 | tf_op jit(solution)/shard_map/scatter-add | solution.py:180
  23.4 3.2 add_select_fusion.1
  26.6 6.0 %scatter-add.90 = f32[26,26,192]{2,0,1:T(8,128)S(1)} dynamic-update-slice(f32[26,26,192]{2,0,1:T(8,128)S(1)} %scatter-add.89, f32[24,24,192]{2,0,1:T(8,128)S(1)} %add_select_fusion.1, s32[]{:T(128)} %bitcast.34, s32[]{:T(128)} %bitcast.35, s32[]{:T(128)} %constant.897.clone.1) | dynamic-update-slice | bytes 884740 | tf_op jit(solution)/shard_map/scatter-add | solution.py:180
  33.9 5.1 scatter-add.91
  40.3 4.9 scatter-add.94
  46.5 4.8 scatter-add.95
  52.6 5.1 scatter-add.96
  59.0 4.9 scatter-add.99
  64.2 4.8 scatter-add.100
  70.9 47.0 %all-gather = bf16[64,24,192]{2,1,0:T(8,128)(2,1)S(1)} all-gather(bf16[4,24,192]{2,1,0:T(8,128)(2,1)S(1)} %pad_maximum_fusion.2), channel_id=2, replica_groups=mesh['face'=2,'sub'=16] {'sub'}, dimensions={0}, use_global_device_ids=true | all-gather | bytes 626688 | tf_op jit(solution)/shard_map/all_gather | solution.py:99
  127.7 39.7 %all-gather.5 = bf16[64,24,192]{2,1,0:T(8,128)(2,1)S(1)} all-gather(bf16[4,24,192]{2,1,0:T(8,128)(2,1)S(1)} %get-tuple-element.537), channel_id=7, replica_groups=mesh['face'=2,'sub'=16] {'sub'}, dimensions={0}, use_global_device_ids=true | all-gather | bytes 626688 | tf_op jit(solution)/shard_map/all_gather | solution.py:139
  181.9 3.8 concatenate.84
  185.7 3.4 convert_reduce_fusion
  196.8 44.8 %all-gather.2 = bf16[64,24,192]{2,1,0:T(8,128)(2,1)} all-gather(bf16[4,24,192]{2,1,0:T(8,128)(2,1)S(1)} %pad_maximum_fusion.3), channel_id=4, replica_groups=mesh['face'=2,'sub'=16] {'sub'}, dimensions={0}, use_global_device_ids=true | all-gather | bytes 626688 | tf_op jit(solution)/shard_map/all_gather | solution.py:99
  250.0 6.1 %scatter-add.110 = f32[26,26,192]{2,0,1:T(8,128)S(1)} dynamic-update-slice(f32[26,26,192]{2,0,1:T(8,128)S(1)} %scatter-add.109, f32[24,24,192]{2,0,1:T(8,128)S(1)} %copy_add_fusion.1, s32[]{:T(128)} %bitcast.3, s32[]{:T(128)} %bitcast.4, s32[]{:T(128)} %constant.897.clone.1) | dynamic-update-slice | bytes 884740 | tf_op jit(solution)/shard_map/scatter-add | solution.py:180
  256.1 3.2 add_select_fusion
  259.2 6.0 %scatter-add.111 = f32[26,26,192]{2,0,1:T(8,128)S(1)} dynamic-update-slice(f32[26,26,192]{2,0,1:T(8,128)S(1)} %scatter-add.110, f32[24,24,192]{2,0,1:T(8,128)S(1)} %add_select_fusion, s32[]{:T(128)} %bitcast.34, s32[]{:T(128)} %bitcast.35, s32[]{:T(128)} %constant.897.clone.1) | dynamic-update-slice | bytes 884740 | tf_op jit(solution)/shard_map/scatter-add | solution.py:180
  266.6 5.1 scatter-add.114
  273.0 4.9 scatter-add.115
  278.1 4.8 scatter-add.116
  283.2 5.1 scatter-add.119
  288.5 4.9 scatter-add.120
  294.9 4.8 scatter-add.121
  306.2 3.8 concatenate.85
  314.6 47.9 %all-gather.7 = bf16[64,24,192]{2,1,0:T(8,128)(2,1)} all-gather(bf16[4,24,192]{2,1,0:T(8,128)(2,1)S(1)} %copy-done.9), channel_id=9, replica_groups=mesh['face'=2,'sub'=16] {'sub'}, dimensions={0}, use_global_device_ids=true | all-gather | bytes 626688 | tf_op jit(solution)/shard_map/all_gather | solution.py:139
  362.5 90.5 %all-reduce.9.cloned.1.call-done = (f32[1728,192]{0,1:T(8,128)}, f32[1728,192]{0,1:T(8,128)}) async-done(((f32[1728,192]{0,1:T(8,128)}, f32[1728,192]{0,1:T(8,128)}), (f32[1728,192]{0,1:T(8,128)}, f32[1728,192]{0,1:T(8,128)})) %all-reduce.9.cloned.1.call-update) | async-done | bytes 2654224 | tf_op jit(solution)/shard_map/psum | solution.py:235
  454.2 2.5 reshape.1470
  470.2 2.1 copy.335
  472.3 2.8 convolution_add_fusion.4
  477.3 40.4 %psum.44 = f32[192]{0:T(256)S(1)} all-reduce(f32[192]{0:T(256)S(1)} %copy-done.34), channel_id=1, replica_groups=mesh['face'=2,'sub'=16] {'sub'}, use_global_device_ids=true, to_apply=%region_7.8 | all-reduce | flops 192 | bytes 1536 | tf_op jit(solution)/shard_map/psum | solution.py:235
  517.7 2.5 psum.45
  (243 shorter events, 96.6 us)
Async XLA Ops:
  7.2 178.5 %copy-start = (bf16[3,3,192,192]{3,2,1,0:T(8,128)(2,1)S(1)}, bf16[3,3,192,192]{3,2,1,0:T(8,128)(2,1)}, u32[]{:S(2)}) copy-start(bf16[3,3,192,192]{3,2,1,0:T(8,128)(2,1)} %param.78) | copy-start | bytes 1990660
  7.2 445.8 %all-reduce.9.cloned.1.call-start = ((), (), s32[]{:S(2)}) async-start(), calls=%async_computation | async-start | bytes 5505024 | tf_op jit(solution)/shard_map/psum | solution.py:235
  63.9 56.0 %copy-start.31 = (s32[32,4]{0,1:T(4,128)S(1)}, s32[32,4]{0,1:T(4,128)}, u32[]{:S(2)}) copy-start(s32[32,4]{0,1:T(4,128)} %param.82) | copy-start | bytes 1540
  63.9 56.0 %copy-start.32 = (s32[4,4]{1,0:T(4,128)S(1)}, s32[4,4]{1,0:T(4,128)}, u32[]{:S(2)}) copy-start(s32[4,4]{1,0:T(4,128)} %constant.917.clone) | copy-start | bytes 196
  64.0 56.0 %copy-start.33 = (s32[4,4]{1,0:T(4,128)S(1)}, s32[4,4]{1,0:T(4,128)}, u32[]{:S(2)}) copy-start(s32[4,4]{1,0:T(4,128)} %constant.918.clone) | copy-start | bytes 196
  64.0 56.6 %copy-start.17 = (s32[32,4]{0,1:T(4,128)S(1)}, s32[32,4]{0,1:T(4,128)}, u32[]{:S(2)}) copy-start(s32[32,4]{0,1:T(4,128)} %param.81) | copy-start | bytes 1540
  69.1 52.2 %copy-start.11 = (bf16[1,24,192]{2,1,0:T(8,128)(2,1)}, bf16[1,24,192]{2,1,0:T(8,128)(2,1)S(1)}, u32[]{:S(2)}) copy-start(bf16[1,24,192]{2,1,0:T(8,128)(2,1)S(1)} %get-tuple-element.496) | copy-start | bytes 27652
  69.1 52.2 %copy-start.12 = (bf16[1,24,192]{2,1,0:T(8,128)(2,1)}, bf16[1,24,192]{2,1,0:T(8,128)(2,1)S(1)}, u32[]{:S(2)}) copy-start(bf16[1,24,192]{2,1,0:T(8,128)(2,1)S(1)} %get-tuple-element.497) | copy-start | bytes 27652
  123.1 46.1 %copy-start.16 = (s32[32,4]{0,1:T(4,128)S(1)}, s32[32,4]{0,1:T(4,128)}, u32[]{:S(2)}) copy-start(s32[32,4]{0,1:T(4,128)} %copy-done.15) | copy-start | bytes 1540
  123.1 46.2 %copy-start.18 = (s32[32,4]{0,1:T(4,128)S(1)}, s32[32,4]{0,1:T(4,128)}, u32[]{:S(2)}) copy-start(s32[32,4]{0,1:T(4,128)} %param.81) | copy-start | bytes 1540
  123.9 3.7 copy-start.25
  124.0 3.7 copy-start.36
  126.8 43.7 %copy-start.19 = (pred[4]{0:T(512)(128)(4,1)}, pred[4]{0:T(512)(128)(4,1)S(1)}, u32[]{:S(2)}) copy-start(pred[4]{0:T(512)(128)(4,1)S(1)} %fusion.27) | copy-start | bytes 16
  175.3 4.8 copy-start.4
  177.3 2.2 copy-start.27
  181.9 3.8 copy-start.39
  288.5 11.2 %copy-start.6 = (bf16[576,192]{1,0:T(8,128)(2,1)S(1)}, bf16[576,192]{1,0:T(8,128)(2,1)}, u32[]{:S(2)}) copy-start(bf16[576,192]{1,0:T(8,128)(2,1)} %copy.330) | copy-start | bytes 663556
  293.4 6.4 %copy-start.3 = (bf16[64,24,192]{2,1,0:T(8,128)(2,1)S(1)}, bf16[64,24,192]{2,1,0:T(8,128)(2,1)}, u32[]{:S(2)}) copy-start(bf16[64,24,192]{2,1,0:T(8,128)(2,1)} %all-gather.2) | copy-start | bytes 1769476
  294.8 5.7 %copy-start.24 = (pred[4]{0:T(512)(128)(4,1)S(1)}, pred[4]{0:T(512)(128)(4,1)}, u32[]{:S(2)}) copy-start(pred[4]{0:T(512)(128)(4,1)} %get-tuple-element.470) | copy-start | bytes 16
  294.8 5.7 %copy-start.26 = (s32[4]{0:T(128)S(1)}, s32[4]{0:T(128)}, u32[]{:S(2)}) copy-start(s32[4]{0:T(128)} %copy-done.25) | copy-start | bytes 52
  294.8 6.0 %copy-start.10 = (bf16[8,24,192]{2,1,0:T(8,128)(2,1)S(1)}, bf16[8,24,192]{2,1,0:T(8,128)(2,1)}, u32[]{:S(2)}) copy-start(bf16[8,24,192]{2,1,0:T(8,128)(2,1)} %all-gather.3) | copy-start | bytes 221188
  294.8 6.1 %copy-start.35 = (pred[4]{0:T(512)(128)(4,1)S(1)}, pred[4]{0:T(512)(128)(4,1)}, u32[]{:S(2)}) copy-start(pred[4]{0:T(512)(128)(4,1)} %get-tuple-element.469) | copy-start | bytes 16
  294.9 6.1 %copy-start.37 = (s32[4]{0:T(128)S(1)}, s32[4]{0:T(128)}, u32[]{:S(2)}) copy-start(s32[4]{0:T(128)} %copy-done.36) | copy-start | bytes 52
  311.8 141.1 %copy-start.28 = (pred[8]{0:T(512)(128)(4,1)S(1)}, pred[8]{0:T(512)(128)(4,1)}, u32[]{:S(2)}) copy-start(pred[8]{0:T(512)(128)(4,1)} %copy-done.27) | copy-start | bytes 28
  311.8 141.1 %copy-start.30 = (s32[8]{0:T(128)S(1)}, s32[8]{0:T(128)}, u32[]{:S(2)}) copy-start(s32[8]{0:T(128)} %copy-done.29) | copy-start | bytes 100
  311.9 209.5 %all-reduce.11.cloned.1.call-start = ((), (), s32[]{:S(2)}) async-start(), calls=%async_computation.1 | async-start | bytes 5505024 | tf_op jit(solution)/shard_map/psum | solution.py:235
  452.9 3.7 copy-start.23
  453.0 11.4 %copy-start.8 = (f32[12,12,192]{2,1,0:T(8,128)S(1)}, f32[12,12,192]{2,1,0:T(8,128)}, u32[]{:S(2)}) copy-start(f32[12,12,192]{2,1,0:T(8,128)} %get-tuple-element.525) | copy-start | bytes 331780
  464.3 5.1 copy-start.5
  465.7 6.6 %copy-start.2 = (bf16[3,3,192,192]{3,2,1,0:T(8,128)(2,1)S(1)}, bf16[3,3,192,192]{3,2,1,0:T(8,128)(2,1)}, u32[]{:S(2)}) copy-start(bf16[3,3,192,192]{3,2,1,0:T(8,128)(2,1)} %param.80) | copy-start | bytes 1990660
  475.1 2.2 copy-start.34
  524.5 3.3 copy-start.1
  (10 other events, 14.9 us)
Sparse Core Ops, SparseCore 0:
  312.0 140.9 all-reduce.8
  455.4 22.2 all-reduce.10
